TPU v7x, 32 devices: a whole 2x2x4 slice. The times are simulated.
32 devices in a mesh: gx: 4 (over y, x), gy: 4 (over z), gz: 2 (over core).
Axes of the slice: x: 2, y: 2, z: 4, core: 2. Of those that a mesh axis runs over, the one named last changes fastest.
Arguments:
- well_sources: float32 [1536, 64], P(('gx', 'gy'), 'gz'), may hold values from -6 to 6
- well_owner: int32 [1536, 1], P(('gx', 'gy')), may hold values from 0 to 15; in each aligned block of 96 rows (0 to 95, 96 to 191, ...) at most 12 rows name the same one
- well_cell: int32 [1536], P(('gx', 'gy')), may hold values from 0 to 2047
- flow_sign: int32 [3, 64, 64, 512], P(None, 'gz', 'gx', 'gy'), may hold values from 0 to 7
- courant: float32 [3, 64, 64, 512], P(None, 'gz', 'gx', 'gy'), may hold values from 0.01 to 0.3
- tracer: float32 [3, 64, 64, 512], P(None, 'gz', 'gx', 'gy'), may hold values from -6 to 6
Outputs:
- lambda_start: float32 [64, 64, 512], P('gz', 'gx', 'gy')
- smoothed: float32 [512, 64, 64], P(('gx', 'gy', 'gz'))
Inputs may be any that keep to these rules, and one draw needn't show every extreme that they name: `well_owner`: among the wells of one index of gx+gy at most 12 name the same owner, a bound that some block of them reaches.
All inputs are finite; a program needn't handle non-finite values.
Results may differ from a plain program's by a relative error of at most 0.00015.
Values sent between devices are 32-bit elements; how exact they have to be, the bound alone decides.
A program may use at most 128 MiB of HBM per device.

v0:
```python
import functools
import math

import jax
import jax.numpy as jnp
from jax import lax
from jax.experimental import pallas as pl
from jax.experimental.pallas import tpu as pltpu
from jax.sharding import PartitionSpec as P

MESH = pl.DeviceIdType.MESH
LANES = 128
ROWS = 8


def round_up(value, unit):
    return -(-value // unit) * unit


def iota(shape, dim):
    return lax.broadcasted_iota(jnp.int32, shape, dim)


def parts(value):
    high = value.astype(jnp.bfloat16)
    return high, (value - high.astype(jnp.float32)).astype(jnp.bfloat16)


def dot(left, right, dims):
    return lax.dot_general(left, right, (dims, ((), ())), preferred_element_type=jnp.float32)


NN = ((1,), (0,))
NT = ((1,), (1,))
TN = ((0,), (0,))


def flag(mask):
    return jnp.where(mask, 1.0, 0.0).astype(jnp.bfloat16)


def dot_three(left, right, dims):
    left_high, left_low = parts(left)
    right_high, right_low = parts(right)
    return (
        dot(left_high, right_high, dims)
        + dot(left_low, right_high, dims)
        + dot(left_high, right_low, dims)
    )


def kernel(
    sizes, source_ref, owner_ref, cell_ref, flow_any, courant_any, tracer_any,
    lambda_ref, wide_ref,
    flow_ref, courant_ref, tracer_ref, load_sem,
    payload_ref, well_send, well_recv, well_send_sem, well_recv_sem,
    rise_ref, fall_ref, sum_ref, grad_ref,
    x_send, x_recv, y_send, y_recv, z_send, z_recv, face_send_sem, face_recv_sem,
    carry_send, carry_recv, carry_send_sem, carry_recv_sem,
    enter_send, enter_recv, enter_send_sem, enter_recv_sem,
    bulk_send, bulk_recv, bulk_send_sem, bulk_recv_sem,
    table_high, table_low,
):
    n_gx, n_gy, n_gz, brick_z, brick_x, brick_y, cap = sizes
    steps = flow_any.shape[0]
    lines = brick_z * brick_x
    groups = n_gx * n_gy
    devices = groups * n_gz
    a, b, c = lax.axis_index("gx"), lax.axis_index("gy"), lax.axis_index("gz")
    group = a * n_gy + b
    me = group * n_gz + c
    wells = source_ref.shape[1]
    full_z = n_gz * brick_z
    full_x = n_gx * brick_x
    wide_x = round_up(full_x, LANES)
    shares = n_gx * n_gz
    y_rows = brick_y // shares
    pad_rows = round_up(y_rows, ROWS)
    tiles = lines // LANES
    tile_z = LANES // brick_x

    courant_load = pltpu.make_async_copy(courant_any, courant_ref, load_sem.at[0, steps])
    courant_load.start()
    flow_loads, tracer_loads = (
        [
            pltpu.make_async_copy(src.at[step], dst.at[step], load_sem.at[kind, step])
            for step in range(steps)
        ]
        for kind, (src, dst) in enumerate(((flow_any, flow_ref), (tracer_any, tracer_ref)))
    )
    for step in reversed(range(steps)):
        flow_loads[step].start()
        tracer_loads[step].start()

    for ref in (x_recv, y_recv, z_recv, carry_recv):
        ref[...] = jnp.zeros_like(ref)

    barrier = pltpu.get_barrier_semaphore()

    def greet(d, carried):
        other = lax.rem(me + d, devices)
        pl.semaphore_signal(
            barrier, inc=1,
            device_id=(
                lax.div(other, n_gy * n_gz), lax.rem(lax.div(other, n_gz), n_gy), lax.rem(other, n_gz)
            ),
            device_id_type=MESH,
        )
        return carried

    lax.fori_loop(1, devices, greet, 0)

    eye = iota((wells, wells), 0) == iota((wells, wells), 1)
    before = iota((wells, wells), 0) < iota((wells, wells), 1)
    owner_row = owner_ref[...].astype(jnp.float32)
    owner_col = jnp.sum(jnp.where(eye, owner_row, 0.0), axis=1, keepdims=True)
    rank_row = jnp.sum(
        jnp.where(before & (owner_col == owner_row), 1.0, 0.0), axis=0, keepdims=True
    )
    slots = groups * cap
    second = rank_row >= cap
    key_row = owner_row * cap + rank_row + jnp.where(second, slots - cap, 0)
    chosen = flag(iota((2 * slots, wells), 0) == key_row.astype(jnp.int32))
    cell_row = cell_ref[...]
    payload_ref[...] = jnp.zeros_like(payload_ref)
    payload_ref[0:brick_z, :] = source_ref[...]
    payload_ref[brick_z:brick_z + 1, :] = lax.div(cell_row, brick_y).astype(jnp.float32)
    payload_ref[brick_z + 1:brick_z + 2, :] = lax.rem(cell_row, brick_y).astype(jnp.float32)
    payload_high, payload_low = parts(payload_ref[...])
    sorted_wells = dot(chosen, payload_high, NT) + dot(chosen, payload_low, NT)
    well_send[...] = sorted_wells[0:slots] + pltpu.roll(sorted_wells[slots:], LANES // 2, 1)

    pl.semaphore_wait(barrier, devices - 1)

    def group_rows(index):
        return pl.ds(pl.multiple_of(index * cap, ROWS), cap)

    def well_copy(d):
        other = lax.rem(group + d, groups)
        return pltpu.make_async_remote_copy(
            src_ref=well_send.at[group_rows(other), :],
            dst_ref=well_recv.at[group_rows(group), :],
            send_sem=well_send_sem.at[d],
            recv_sem=well_recv_sem.at[d],
            device_id=(lax.div(other, n_gy), lax.rem(other, n_gy), c),
            device_id_type=MESH,
        )

    def well_start(d, carried):
        well_copy(d).start()
        return carried

    lax.fori_loop(1, groups, well_start, 0)
    well_recv[group_rows(group), :] = well_send[group_rows(group), :]

    shape = (n_gx * LANES, wide_x)
    at_x = lax.div(iota(shape, 0), LANES) * brick_x + lax.rem(iota(shape, 0), brick_x)
    far = jnp.abs(at_x - iota(shape, 1)).astype(jnp.float32)
    table = jnp.exp(far * (-0.5 / brick_x)) / math.sqrt(2 * brick_x) / math.sqrt(2 * brick_z)
    table = jnp.where(iota(shape, 1) < full_x, table, 0.0)
    depth_of = lax.rem(lax.div(iota(shape, 0), brick_x), tile_z)
    for depth in range(tile_z):
        high, low = parts(jnp.where(depth_of == depth, table, 0.0))
        table_high[:, depth * wide_x:(depth + 1) * wide_x] = high
        table_low[:, depth * wide_x:(depth + 1) * wide_x] = low

    spread = flag(lax.div(iota((lines, LANES), 0), brick_x) == iota((lines, LANES), 1))
    x_pick = flag(iota((ROWS, LANES), 1) == brick_z)

    courant_load.wait()

    def well_wait(d, carried):
        well_copy(d).wait_recv()
        return carried

    def well_sent(d, carried):
        well_copy(d).wait_send()
        return carried

    lax.fori_loop(1, groups, well_wait, 0)
    landed = well_recv[...]
    landed = jnp.concatenate([landed, pltpu.roll(landed, LANES // 2, 1)], axis=0)
    landed_high, landed_low = parts(landed)
    x_row = dot(x_pick, landed_high, NT)[0:1, :].astype(jnp.int32)
    x_hit = lax.rem(iota((lines, 2 * slots), 0), brick_x) == x_row
    y_hit = flag(
        iota((2 * slots, LANES), 1) == landed[:, brick_z + 1:brick_z + 2].astype(jnp.int32)
    )
    spread_high = jnp.where(x_hit, dot(spread, landed_high, NT), 0.0).astype(jnp.bfloat16)
    spread_low = jnp.where(x_hit, dot(spread, landed_low, NT), 0.0).astype(jnp.bfloat16)
    adjoint = dot(spread_high, y_hit, NN) + dot(spread_low, y_hit, NN)

    y_pos = iota((lines, brick_y), 1)
    x_pos = lax.rem(iota((lines, brick_y), 0), brick_x)
    take_row, take_lane = iota((2 * ROWS, brick_y), 0), iota((2 * ROWS, brick_y), 1)
    take = flag(
        ((take_row < ROWS) & (take_lane == 0)) | ((take_row >= ROWS) & (take_lane == brick_y - 1))
    )
    put = flag(
        ((take_row == 0) & (take_lane == brick_y - 1)) | ((take_row == ROWS) & (take_lane == 0))
    )

    def face_copies(step):
        copies = []
        for axis, (place, count, send, recv) in enumerate(
            ((a, n_gx, x_send, x_recv), (b, n_gy, y_send, y_recv), (c, n_gz, z_send, z_recv))
        ):
            for side in range(2):
                moved = place - 1 if side == 0 else place + 1
                target = [a, b, c]
                target[axis] = lax.rem(moved + count, count)
                sends = place > 0 if side == 0 else place < count - 1
                gets = place < count - 1 if side == 0 else place > 0
                copy = pltpu.make_async_remote_copy(
                    src_ref=send.at[step, side],
                    dst_ref=recv.at[step, side],
                    send_sem=face_send_sem.at[step, axis, side],
                    recv_sem=face_recv_sem.at[step, axis, side],
                    device_id=tuple(target),
                    device_id_type=MESH,
                )
                copies.append((copy, sends, gets))
        return copies

    def when_start(copy, sends):
        @pl.when(sends)
        def _():
            copy.start()

    all_copies = []
    for step in reversed(range(steps)):
        copies = face_copies(step)
        all_copies.extend(copies)
        flow_loads[step].wait()
        flow = flow_ref[step]
        flows = [courant_ref[axis] * adjoint for axis in range(3)]
        rise = [
            jnp.where((flow & (1 << axis)) != 0, flows[axis], 0.0) for axis in range(3)
        ]
        fall = [flows[axis] - rise[axis] for axis in range(3)]
        z_send[step, 0] = rise[2][0:brick_x]
        z_send[step, 1] = fall[2][lines - brick_x:lines]
        when_start(*copies[4][:2])
        when_start(*copies[5][:2])
        rise_ref[...] = rise[0]
        fall_ref[...] = fall[0]
        x_send[step, 0] = rise_ref[pl.ds(0, brick_z, stride=brick_x), :]
        x_send[step, 1] = fall_ref[pl.ds(brick_x - 1, brick_z, stride=brick_x), :]
        when_start(*copies[0][:2])
        when_start(*copies[1][:2])
        edge = jnp.where(y_pos == 0, rise[1], jnp.where(y_pos == brick_y - 1, fall[1], 0.0))
        edge_high, edge_low = parts(edge)
        edge_rows = dot(take, edge_high, NT) + dot(take, edge_low, NT)
        y_send[step, 0] = edge_rows[0:ROWS]
        y_send[step, 1] = edge_rows[ROWS:2 * ROWS]
        when_start(*copies[2][:2])
        when_start(*copies[3][:2])

        rest = 1.0 - (courant_ref[0] + courant_ref[1] + courant_ref[2])
        updated = rest * adjoint
        updated = updated + jnp.where(
            x_pos == brick_x - 1, 0.0, pltpu.roll(rise[0], lines - 1, 0)
        )
        updated = updated + jnp.where(x_pos == 0, 0.0, pltpu.roll(fall[0], 1, 0))
        updated = updated + jnp.where(
            y_pos == brick_y - 1, 0.0, pltpu.roll(rise[1], brick_y - 1, 1)
        )
        updated = updated + jnp.where(y_pos == 0, 0.0, pltpu.roll(fall[1], 1, 1))
        border = jnp.zeros((brick_x, brick_y), jnp.float32)
        updated = updated + jnp.concatenate([rise[2][brick_x:], border], axis=0)
        updated = updated + jnp.concatenate([border, fall[2][:lines - brick_x]], axis=0)
        sum_ref[...] = updated

        for copy, _, gets in copies:
            @pl.when(gets)
            def _():
                copy.wait_recv()

        top = pl.ds(brick_x - 1, brick_z, stride=brick_x)
        bottom = pl.ds(0, brick_z, stride=brick_x)
        sum_ref[top, :] = sum_ref[top, :] + x_recv[step, 0]
        sum_ref[bottom, :] = sum_ref[bottom, :] + x_recv[step, 1]
        last = pl.ds(lines - brick_x, brick_x)
        sum_ref[last, :] = sum_ref[last, :] + z_recv[step, 0]
        first = pl.ds(0, brick_x)
        sum_ref[first, :] = sum_ref[first, :] + z_recv[step, 1]
        side_rows = jnp.concatenate([y_recv[step, 0], y_recv[step, 1]], axis=0)
        side_high, side_low = parts(side_rows)
        adjoint = sum_ref[...] + (dot(side_high, put, TN) + dot(side_low, put, TN))
        tracer_loads[step].wait()
        if step == steps - 1:
            gradient = adjoint * tracer_ref[step]
        else:
            gradient = grad_ref[...] + adjoint * tracer_ref[step]
        grad_ref[...] = gradient

    length = 2.0 * brick_y
    from_end = jnp.where(take_row < ROWS, brick_y - take_lane, take_lane + 1)
    pull = jnp.exp(from_end.astype(jnp.float32) * (-1.0 / length)) / math.sqrt(length)
    carries = dot_three(pull, gradient, NT)
    packed = [
        carries[row:row + 1, t * LANES:(t + 1) * LANES] for row in (0, ROWS) for t in range(tiles)
    ]
    carry_send[...] = jnp.concatenate(packed, axis=0)
    carry_copies = []
    for d in range(1, n_gy):
        for moved, back in ((b + d, b - d), (b - d, b + d)):
            copy = pltpu.make_async_remote_copy(
                src_ref=carry_send,
                dst_ref=carry_recv.at[b],
                send_sem=carry_send_sem.at[lax.rem(moved + n_gy, n_gy)],
                recv_sem=carry_recv_sem.at[b],
                device_id=(a, lax.rem(moved + n_gy, n_gy), c),
                device_id_type=MESH,
            )
            arrival = pltpu.make_async_remote_copy(
                src_ref=carry_send,
                dst_ref=carry_recv.at[lax.rem(back + n_gy, n_gy)],
                send_sem=carry_send_sem.at[lax.rem(back + n_gy, n_gy)],
                recv_sem=carry_recv_sem.at[lax.rem(back + n_gy, n_gy)],
                device_id=(a, lax.rem(moved + n_gy, n_gy), c),
                device_id_type=MESH,
            )
            sends = (moved >= 0) & (moved < n_gy)
            gets = (back >= 0) & (back < n_gy)
            when_start(copy, sends)
            carry_copies.append((copy, sends, arrival, gets))

    def line_place(row):
        return lax.div(row, pad_rows) * y_rows + lax.rem(row, pad_rows)

    shape = (shares * pad_rows, brick_y)
    near = jnp.abs(line_place(iota(shape, 0)) - iota(shape, 1)).astype(jnp.float32)
    table_y = jnp.exp(near * (-1.0 / length)) / math.sqrt(length)
    bulk_send[...] = dot_three(table_y, gradient, NT)

    mine = a * n_gz + c

    def bulk_copy(d):
        share = lax.rem(mine + d, shares)
        other = b * shares + share
        return other, pltpu.make_async_remote_copy(
            src_ref=bulk_send.at[pl.ds(pl.multiple_of(share * pad_rows, ROWS), pad_rows), :],
            dst_ref=bulk_recv.at[mine],
            send_sem=bulk_send_sem.at[share],
            recv_sem=bulk_recv_sem.at[mine],
            device_id=(
                lax.div(other, n_gy * n_gz), lax.rem(lax.div(other, n_gz), n_gy), lax.rem(other, n_gz)
            ),
            device_id_type=MESH,
        )

    def bulk_start(d, carried):
        other, copy = bulk_copy(d)

        @pl.when(other != me)
        def _():
            copy.start()

        return carried

    lax.fori_loop(0, shares, bulk_start, 0)
    lambda_ref[...] = adjoint

    own = lax.div(me, shares) == b

    @pl.when(own)
    def _():
        rows = pl.ds(pl.multiple_of((me - b * shares) * pad_rows, ROWS), pad_rows)
        bulk_recv[mine] = bulk_send[rows, :]

    for _, _, arrival, gets in carry_copies:
        @pl.when(gets)
        def _():
            arrival.wait_recv()

    carry_row = iota((2 * tiles, LANES), 0)
    entering = jnp.zeros((2 * tiles, LANES), jnp.float32)
    for brick in range(n_gy):
        between = jnp.where(carry_row < tiles, b - brick - 1, brick - b - 1)
        weight = jnp.exp(jnp.maximum(between, 0).astype(jnp.float32) * (-brick_y / length))
        entering = entering + jnp.where(between >= 0, weight, 0.0) * carry_recv[brick]
    enter_send[...] = entering

    def enter_copy(d):
        share = lax.rem(mine + d, shares)
        other = b * shares + share
        return other, pltpu.make_async_remote_copy(
            src_ref=enter_send,
            dst_ref=enter_recv.at[mine],
            send_sem=enter_send_sem.at[share],
            recv_sem=enter_recv_sem.at[mine],
            device_id=(
                lax.div(other, n_gy * n_gz), lax.rem(lax.div(other, n_gz), n_gy), lax.rem(other, n_gz)
            ),
            device_id_type=MESH,
        )

    def enter_start(d, carried):
        other, copy = enter_copy(d)

        @pl.when(other != me)
        def _():
            copy.start()

        return carried

    lax.fori_loop(0, shares, enter_start, 0)

    @pl.when(own)
    def _():
        enter_recv[mine] = enter_send[...]

    for copy, sends, _ in all_copies:
        @pl.when(sends)
        def _():
            copy.wait_send()

    for copy, sends, _, _ in carry_copies:
        @pl.when(sends)
        def _():
            copy.wait_send()

    at_y = lax.rem(me, shares) * y_rows + iota((pad_rows, LANES), 0)
    from_low = jnp.exp(at_y.astype(jnp.float32) * (-1.0 / length))
    from_high = jnp.exp(jnp.maximum(brick_y - 1 - at_y, 0).astype(jnp.float32) * (-1.0 / length))
    for i in range(n_gx):
        for k in range(n_gz):
            slot = i * n_gz + k

            @pl.when(jnp.logical_not(own & (mine == slot)))
            def _():
                for send, recv, send_sem, recv_sem in (
                    (bulk_send.at[pl.ds(0, pad_rows), :], bulk_recv, bulk_send_sem, bulk_recv_sem),
                    (enter_send, enter_recv, enter_send_sem, enter_recv_sem),
                ):
                    pltpu.make_async_remote_copy(
                        src_ref=send,
                        dst_ref=recv.at[slot],
                        send_sem=send_sem.at[slot],
                        recv_sem=recv_sem.at[slot],
                        device_id=(a, b, c),
                        device_id_type=MESH,
                    ).wait_recv()

        rows = []
        for k in range(n_gz):
            slot = i * n_gz + k
            for t in range(tiles):
                rows.append(
                    bulk_recv[slot, :, t * LANES:(t + 1) * LANES]
                    + from_low * enter_recv[slot, t:t + 1, :]
                    + from_high * enter_recv[slot, tiles + t:tiles + t + 1, :]
                )
        high, low = parts(jnp.concatenate(rows, axis=0))
        block_high = table_high[i * LANES:(i + 1) * LANES, :]
        block_low = table_low[i * LANES:(i + 1) * LANES, :]
        product = dot(high, block_high, NN) + dot(low, block_high, NN) + dot(high, block_low, NN)
        wide_ref[...] = product if i == 0 else wide_ref[...] + product

    def bulk_sent(d, carried):
        other, copy = bulk_copy(d)
        _, enter = enter_copy(d)

        @pl.when(other != me)
        def _():
            copy.wait_send()
            enter.wait_send()

        return carried

    lax.fori_loop(0, shares, bulk_sent, 0)
    lax.fori_loop(1, groups, well_sent, 0)


def depth_kernel(
    sizes, lambda_ref, wide_ref, lambda_out, smooth_ref, stage_ref=None
):
    brick_z, full_z, full_x, y_rows, pad_rows, tile_z = sizes
    wide_x = round_up(full_x, LANES)
    lambda_out[...] = lambda_ref[...]

    fade = math.exp(-0.5 / brick_z)

    def plane(z):
        row, depth = z // tile_z * pad_rows, z % tile_z
        return wide_ref[row:row + y_rows, depth * wide_x:(depth + 1) * wide_x]

    ahead = [plane(0)]
    for z in range(1, full_z):
        ahead.append(plane(z) + fade * ahead[-1])
    behind = None
    for z in reversed(range(full_z)):
        total = ahead[z] if behind is None else ahead[z] + behind
        if full_x <= LANES:
            smooth_ref[pl.ds(z, y_rows, stride=full_z), :] = total[:, 0:full_x]
        else:
            for tile in range(wide_x // LANES):
                part = total[:, tile * LANES:(tile + 1) * LANES]
                stage_ref[tile, pl.ds(z, y_rows, stride=full_z), :] = part
        behind = fade * (plane(z) if behind is None else plane(z) + behind)

    if full_x > LANES:
        for tile in range(wide_x // LANES):
            end = min((tile + 1) * LANES, full_x)
            smooth_ref[:, tile * LANES:end] = stage_ref[tile][:, 0:end - tile * LANES]


def per_device(well_sources, well_owner, well_cell, flow_sign, courant, tracer):
    steps, brick_z, brick_x, brick_y = tracer.shape
    n_gx, n_gy, n_gz = lax.axis_size("gx"), lax.axis_size("gy"), lax.axis_size("gz")
    groups, shares = n_gx * n_gy, n_gx * n_gz
    wells = well_cell.shape[0]
    cap = round_up(-(-wells // groups), ROWS)
    lines = brick_z * brick_x
    y_rows = brick_y // shares
    pad_rows = round_up(y_rows, ROWS)
    full_x, full_z = n_gx * brick_x, n_gz * brick_z
    wide_x = round_up(full_x, LANES)
    tile_z = LANES // brick_x
    tiles = lines // LANES
    f32 = jnp.float32
    sizes = (n_gx, n_gy, n_gz, brick_z, brick_x, brick_y, cap)
    dma = pltpu.SemaphoreType.DMA
    vmem = pl.BlockSpec(memory_space=pltpu.VMEM)
    away = pl.BlockSpec(memory_space=pl.ANY)
    field = (3, lines, brick_y)
    stage = []
    if full_x > LANES:
        stage = [pltpu.VMEM((wide_x // LANES, y_rows * full_z, LANES), f32)]
    run = pl.pallas_call(
        functools.partial(kernel, sizes),
        out_shape=(
            jax.ShapeDtypeStruct((lines, brick_y), f32),
            jax.ShapeDtypeStruct((n_gz * tiles * pad_rows, tile_z * wide_x), f32),
        ),
        in_specs=[vmem, vmem, vmem, away, away, away],
        out_specs=(vmem, vmem),
        scratch_shapes=[
            pltpu.VMEM((steps, lines, brick_y), jnp.int32),
            pltpu.VMEM(field, f32),
            pltpu.VMEM((steps, lines, brick_y), f32),
            dma((2, steps + 1)),
            pltpu.VMEM((LANES, wells), f32),
            pltpu.VMEM((groups * cap, LANES), f32),
            pltpu.VMEM((groups * cap, LANES), f32),
            dma((groups,)),
            dma((groups,)),
            pltpu.VMEM((lines, brick_y), f32),
            pltpu.VMEM((lines, brick_y), f32),
            pltpu.VMEM((lines, brick_y), f32),
            pltpu.VMEM((lines, brick_y), f32),
            pltpu.VMEM((steps, 2, brick_z, brick_y), f32),
            pltpu.VMEM((steps, 2, brick_z, brick_y), f32),
            pltpu.VMEM((steps, 2, ROWS, lines), f32),
            pltpu.VMEM((steps, 2, ROWS, lines), f32),
            pltpu.VMEM((steps, 2, brick_x, brick_y), f32),
            pltpu.VMEM((steps, 2, brick_x, brick_y), f32),
            dma((steps, 3, 2)),
            dma((steps, 3, 2)),
            pltpu.VMEM((2 * tiles, LANES), f32),
            pltpu.VMEM((n_gy, 2 * tiles, LANES), f32),
            dma((n_gy,)),
            dma((n_gy,)),
            pltpu.VMEM((2 * tiles, LANES), f32),
            pltpu.VMEM((shares, 2 * tiles, LANES), f32),
            dma((shares,)),
            dma((shares,)),
            pltpu.VMEM((shares * pad_rows, lines), f32),
            pltpu.VMEM((shares, pad_rows, lines), f32),
            dma((shares,)),
            dma((shares,)),
            pltpu.VMEM((n_gx * LANES, tile_z * wide_x), jnp.bfloat16),
            pltpu.VMEM((n_gx * LANES, tile_z * wide_x), jnp.bfloat16),
        ],
        compiler_params=pltpu.CompilerParams(
            collective_id=0, has_side_effects=True, vmem_limit_bytes=56 * 2**20
        ),
    )
    start, wide = run(
        well_sources.T,
        well_owner.reshape(1, wells),
        well_cell.reshape(1, wells),
        flow_sign.reshape(steps, lines, brick_y),
        courant.reshape(field),
        tracer.reshape(steps, lines, brick_y),
    )
    depth_sizes = (brick_z, full_z, full_x, y_rows, pad_rows, tile_z)
    start, smoothed = pl.pallas_call(
        functools.partial(depth_kernel, depth_sizes),
        out_shape=(
            jax.ShapeDtypeStruct((lines, brick_y), f32),
            jax.ShapeDtypeStruct((y_rows * full_z, full_x), f32),
        ),
        in_specs=[vmem, vmem],
        out_specs=(vmem, vmem),
        scratch_shapes=stage,
    )(start, wide)
    return (
        start.reshape(brick_z, brick_x, brick_y),
        smoothed.reshape(y_rows, full_z, full_x),
    )


def solution(mesh):
    return jax.shard_map(
        per_device,
        mesh=mesh,
        in_specs=(
            P(("gx", "gy"), "gz"),
            P(("gx", "gy"), None),
            P(("gx", "gy")),
            P(None, "gz", "gx", "gy"),
            P(None, "gz", "gx", "gy"),
            P(None, "gz", "gx", "gy"),
        ),
        out_specs=(P("gz", "gx", "gy"), P(("gx", "gy", "gz"), None, None)),
        check_vma=False,
    )
```

profile of v0, /device:TPU:0, one launch (start us, length us, event | category | flops | bytes accessed | tf_op | source)
XLA Modules:
  0.0 38.5 jit_solution(16469920739775934424)
XLA Ops:
  0.6 35.5 %shard_map.77 = (f32[512,128]{1,0:T(8,128)}, f32[128,1024]{1,0:T(8,128)}) custom-call(f32[32,96]{1,0:T(8,128)} %bitcast.11, s32[1,96]{1,0:T(1,128)} %bitcast.12, s32[1,96]{1,0:T(1,128)} %bitcast.13, s32[3,512,128]{2,1,0:T(8,128)} %bitcast.8, f32[3,512,128]{2,1,0:T(8,128)} %bitcast.9, f32[3,512,128]{2,1,0:T(8,128)} %bitcast.10), custom_call_target="tpu_custom_call" | custom-call | tf_op jit(solution)/shard_map/pallas_call | solution.py:580
  36.1 2.4 %shard_map.78 = (f32[512,128]{1,0:T(8,128)}, f32[1024,64]{1,0:T(8,128)}) custom-call(f32[512,128]{1,0:T(8,128)} %get-tuple-element.6.lambda_ref, f32[128,1024]{1,0:T(8,128)} %get-tuple-element.7.wide_ref), custom_call_target="tpu_custom_call" | custom-call | tf_op jit(solution)/shard_map/pallas_call | solution.py:589
where the time goes:
time: 38.7 us; the launch traced here: 38.5 us
  Pallas kernels  37.9 us (98%)
  between operations  0.64 us (2%)
    pallas_call x1, Pallas kernels, per_device(): run(well_sources.T, well_owner.reshape(1, wells), well_cell.reshape(1, we...  35.5 us
    pallas_call x1, Pallas kernels, per_device(): pl.pallas_call(functools.partial(depth_kernel, depth_sizes), out_shape=(j...  2.37 us

commit v1 on v0

--- a/solution.py
+++ b/solution.py
@@ -19,6 +19,22 @@
 
 def iota(shape, dim):
     return lax.broadcasted_iota(jnp.int32, shape, dim)
+
+
+def div(value, by):
+    return value >> (by.bit_length() - 1) if by & (by - 1) == 0 else lax.div(value, by)
+
+
+def rem(value, by):
+    return value & (by - 1) if by & (by - 1) == 0 else lax.rem(value, by)
+
+
+def each(start, stop, act):
+    if stop - start <= 32:
+        for i in range(start, stop):
+            act(i)
+    else:
+        lax.fori_loop(start, stop, lambda i, carried: (act(i), carried)[1], 0)
 
 
 def parts(value):
@@ -50,8 +66,9 @@
 
 
 def kernel(
-    sizes, source_ref, owner_ref, cell_ref, flow_any, courant_any, tracer_any,
-    lambda_ref, wide_ref,
+    sizes, source_any, owner_any, cell_any, flow_any, courant_any, tracer_any,
+    lambda_any, wide_ref, lambda_ref, lambda_sem,
+    source_ref, owner_ref, cell_ref, small_sem,
     flow_ref, courant_ref, tracer_ref, load_sem,
     payload_ref, well_send, well_recv, well_send_sem, well_recv_sem,
     rise_ref, fall_ref, sum_ref, grad_ref,
@@ -59,17 +76,18 @@
     carry_send, carry_recv, carry_send_sem, carry_recv_sem,
     enter_send, enter_recv, enter_send_sem, enter_recv_sem,
     bulk_send, bulk_recv, bulk_send_sem, bulk_recv_sem,
-    table_high, table_low,
+    table_high, table_low, y_high, y_low,
 ):
     n_gx, n_gy, n_gz, brick_z, brick_x, brick_y, cap = sizes
     steps = flow_any.shape[0]
+    length = 2.0 * brick_y
     lines = brick_z * brick_x
     groups = n_gx * n_gy
     devices = groups * n_gz
     a, b, c = lax.axis_index("gx"), lax.axis_index("gy"), lax.axis_index("gz")
     group = a * n_gy + b
     me = group * n_gz + c
-    wells = source_ref.shape[1]
+    wells = source_any.shape[1]
     full_z = n_gz * brick_z
     full_x = n_gx * brick_x
     wide_x = round_up(full_x, LANES)
@@ -79,6 +97,30 @@
     tiles = lines // LANES
     tile_z = LANES // brick_x
 
+    for ref in (x_recv, y_recv, z_recv, carry_recv):
+        ref[...] = jnp.zeros_like(ref)
+
+    barrier = pltpu.get_barrier_semaphore()
+
+    def greet(d):
+        other = rem(me + d, devices)
+        pl.semaphore_signal(
+            barrier, inc=1,
+            device_id=(
+                div(other, n_gy * n_gz), rem(div(other, n_gz), n_gy), rem(other, n_gz)
+            ),
+            device_id_type=MESH,
+        )
+
+    each(1, devices, greet)
+    small_loads = [
+        pltpu.make_async_copy(src, dst, small_sem.at[i])
+        for i, (src, dst) in enumerate(
+            ((owner_any, owner_ref), (cell_any, cell_ref), (source_any, source_ref))
+        )
+    ]
+    for load in small_loads:
+        load.start()
     courant_load = pltpu.make_async_copy(courant_any, courant_ref, load_sem.at[0, steps])
     courant_load.start()
     flow_loads, tracer_loads = (
@@ -92,26 +134,10 @@
         flow_loads[step].start()
         tracer_loads[step].start()
 
-    for ref in (x_recv, y_recv, z_recv, carry_recv):
-        ref[...] = jnp.zeros_like(ref)
-
-    barrier = pltpu.get_barrier_semaphore()
-
-    def greet(d, carried):
-        other = lax.rem(me + d, devices)
-        pl.semaphore_signal(
-            barrier, inc=1,
-            device_id=(
-                lax.div(other, n_gy * n_gz), lax.rem(lax.div(other, n_gz), n_gy), lax.rem(other, n_gz)
-            ),
-            device_id_type=MESH,
-        )
-        return carried
-
-    lax.fori_loop(1, devices, greet, 0)
-
     eye = iota((wells, wells), 0) == iota((wells, wells), 1)
     before = iota((wells, wells), 0) < iota((wells, wells), 1)
+    for load in small_loads:
+        load.wait()
     owner_row = owner_ref[...].astype(jnp.float32)
     owner_col = jnp.sum(jnp.where(eye, owner_row, 0.0), axis=1, keepdims=True)
     rank_row = jnp.sum(
@@ -124,8 +150,8 @@
     cell_row = cell_ref[...]
     payload_ref[...] = jnp.zeros_like(payload_ref)
     payload_ref[0:brick_z, :] = source_ref[...]
-    payload_ref[brick_z:brick_z + 1, :] = lax.div(cell_row, brick_y).astype(jnp.float32)
-    payload_ref[brick_z + 1:brick_z + 2, :] = lax.rem(cell_row, brick_y).astype(jnp.float32)
+    payload_ref[brick_z:brick_z + 1, :] = div(cell_row, brick_y).astype(jnp.float32)
+    payload_ref[brick_z + 1:brick_z + 2, :] = rem(cell_row, brick_y).astype(jnp.float32)
     payload_high, payload_low = parts(payload_ref[...])
     sorted_wells = dot(chosen, payload_high, NT) + dot(chosen, payload_low, NT)
     well_send[...] = sorted_wells[0:slots] + pltpu.roll(sorted_wells[slots:], LANES // 2, 1)
@@ -136,53 +162,58 @@
         return pl.ds(pl.multiple_of(index * cap, ROWS), cap)
 
     def well_copy(d):
-        other = lax.rem(group + d, groups)
+        other = rem(group + d, groups)
         return pltpu.make_async_remote_copy(
             src_ref=well_send.at[group_rows(other), :],
             dst_ref=well_recv.at[group_rows(group), :],
             send_sem=well_send_sem.at[d],
             recv_sem=well_recv_sem.at[d],
-            device_id=(lax.div(other, n_gy), lax.rem(other, n_gy), c),
+            device_id=(div(other, n_gy), rem(other, n_gy), c),
             device_id_type=MESH,
         )
 
-    def well_start(d, carried):
+    def well_start(d):
         well_copy(d).start()
-        return carried
-
-    lax.fori_loop(1, groups, well_start, 0)
+
+    each(1, groups, well_start)
     well_recv[group_rows(group), :] = well_send[group_rows(group), :]
 
     shape = (n_gx * LANES, wide_x)
-    at_x = lax.div(iota(shape, 0), LANES) * brick_x + lax.rem(iota(shape, 0), brick_x)
+    at_x = div(iota(shape, 0), LANES) * brick_x + rem(iota(shape, 0), brick_x)
     far = jnp.abs(at_x - iota(shape, 1)).astype(jnp.float32)
     table = jnp.exp(far * (-0.5 / brick_x)) / math.sqrt(2 * brick_x) / math.sqrt(2 * brick_z)
     table = jnp.where(iota(shape, 1) < full_x, table, 0.0)
-    depth_of = lax.rem(lax.div(iota(shape, 0), brick_x), tile_z)
+    depth_of = rem(div(iota(shape, 0), brick_x), tile_z)
     for depth in range(tile_z):
         high, low = parts(jnp.where(depth_of == depth, table, 0.0))
         table_high[:, depth * wide_x:(depth + 1) * wide_x] = high
         table_low[:, depth * wide_x:(depth + 1) * wide_x] = low
 
-    spread = flag(lax.div(iota((lines, LANES), 0), brick_x) == iota((lines, LANES), 1))
+    def line_place(row):
+        return div(row, pad_rows) * y_rows + rem(row, pad_rows)
+
+    shape = (shares * pad_rows, brick_y)
+    near = jnp.abs(line_place(iota(shape, 0)) - iota(shape, 1)).astype(jnp.float32)
+    table_y = jnp.exp(near * (-1.0 / length)) / math.sqrt(length)
+    y_high[...], y_low[...] = parts(table_y)
+
+    spread = flag(div(iota((lines, LANES), 0), brick_x) == iota((lines, LANES), 1))
     x_pick = flag(iota((ROWS, LANES), 1) == brick_z)
 
     courant_load.wait()
 
-    def well_wait(d, carried):
+    def well_wait(d):
         well_copy(d).wait_recv()
-        return carried
-
-    def well_sent(d, carried):
+
+    def well_sent(d):
         well_copy(d).wait_send()
-        return carried
-
-    lax.fori_loop(1, groups, well_wait, 0)
+
+    each(1, groups, well_wait)
     landed = well_recv[...]
     landed = jnp.concatenate([landed, pltpu.roll(landed, LANES // 2, 1)], axis=0)
     landed_high, landed_low = parts(landed)
     x_row = dot(x_pick, landed_high, NT)[0:1, :].astype(jnp.int32)
-    x_hit = lax.rem(iota((lines, 2 * slots), 0), brick_x) == x_row
+    x_hit = rem(iota((lines, 2 * slots), 0), brick_x) == x_row
     y_hit = flag(
         iota((2 * slots, LANES), 1) == landed[:, brick_z + 1:brick_z + 2].astype(jnp.int32)
     )
@@ -191,7 +222,7 @@
     adjoint = dot(spread_high, y_hit, NN) + dot(spread_low, y_hit, NN)
 
     y_pos = iota((lines, brick_y), 1)
-    x_pos = lax.rem(iota((lines, brick_y), 0), brick_x)
+    x_pos = rem(iota((lines, brick_y), 0), brick_x)
     take_row, take_lane = iota((2 * ROWS, brick_y), 0), iota((2 * ROWS, brick_y), 1)
     take = flag(
         ((take_row < ROWS) & (take_lane == 0)) | ((take_row >= ROWS) & (take_lane == brick_y - 1))
@@ -208,7 +239,7 @@
             for side in range(2):
                 moved = place - 1 if side == 0 else place + 1
                 target = [a, b, c]
-                target[axis] = lax.rem(moved + count, count)
+                target[axis] = rem(moved + count, count)
                 sends = place > 0 if side == 0 else place < count - 1
                 gets = place < count - 1 if side == 0 else place > 0
                 copy = pltpu.make_async_remote_copy(
@@ -294,7 +325,6 @@
             gradient = grad_ref[...] + adjoint * tracer_ref[step]
         grad_ref[...] = gradient
 
-    length = 2.0 * brick_y
     from_end = jnp.where(take_row < ROWS, brick_y - take_lane, take_lane + 1)
     pull = jnp.exp(from_end.astype(jnp.float32) * (-1.0 / length)) / math.sqrt(length)
     carries = dot_three(pull, gradient, NT)
@@ -308,17 +338,17 @@
             copy = pltpu.make_async_remote_copy(
                 src_ref=carry_send,
                 dst_ref=carry_recv.at[b],
-                send_sem=carry_send_sem.at[lax.rem(moved + n_gy, n_gy)],
+                send_sem=carry_send_sem.at[rem(moved + n_gy, n_gy)],
                 recv_sem=carry_recv_sem.at[b],
-                device_id=(a, lax.rem(moved + n_gy, n_gy), c),
+                device_id=(a, rem(moved + n_gy, n_gy), c),
                 device_id_type=MESH,
             )
             arrival = pltpu.make_async_remote_copy(
                 src_ref=carry_send,
-                dst_ref=carry_recv.at[lax.rem(back + n_gy, n_gy)],
-                send_sem=carry_send_sem.at[lax.rem(back + n_gy, n_gy)],
-                recv_sem=carry_recv_sem.at[lax.rem(back + n_gy, n_gy)],
-                device_id=(a, lax.rem(moved + n_gy, n_gy), c),
+                dst_ref=carry_recv.at[rem(back + n_gy, n_gy)],
+                send_sem=carry_send_sem.at[rem(back + n_gy, n_gy)],
+                recv_sem=carry_recv_sem.at[rem(back + n_gy, n_gy)],
+                device_id=(a, rem(moved + n_gy, n_gy), c),
                 device_id_type=MESH,
             )
             sends = (moved >= 0) & (moved < n_gy)
@@ -326,18 +356,15 @@
             when_start(copy, sends)
             carry_copies.append((copy, sends, arrival, gets))
 
-    def line_place(row):
-        return lax.div(row, pad_rows) * y_rows + lax.rem(row, pad_rows)
-
-    shape = (shares * pad_rows, brick_y)
-    near = jnp.abs(line_place(iota(shape, 0)) - iota(shape, 1)).astype(jnp.float32)
-    table_y = jnp.exp(near * (-1.0 / length)) / math.sqrt(length)
-    bulk_send[...] = dot_three(table_y, gradient, NT)
+    high, low = parts(gradient)
+    bulk_send[...] = (
+        dot(y_high[...], high, NT) + dot(y_low[...], high, NT) + dot(y_high[...], low, NT)
+    )
 
     mine = a * n_gz + c
 
     def bulk_copy(d):
-        share = lax.rem(mine + d, shares)
+        share = rem(mine + d, shares)
         other = b * shares + share
         return other, pltpu.make_async_remote_copy(
             src_ref=bulk_send.at[pl.ds(pl.multiple_of(share * pad_rows, ROWS), pad_rows), :],
@@ -345,24 +372,24 @@
             send_sem=bulk_send_sem.at[share],
             recv_sem=bulk_recv_sem.at[mine],
             device_id=(
-                lax.div(other, n_gy * n_gz), lax.rem(lax.div(other, n_gz), n_gy), lax.rem(other, n_gz)
+                div(other, n_gy * n_gz), rem(div(other, n_gz), n_gy), rem(other, n_gz)
             ),
             device_id_type=MESH,
         )
 
-    def bulk_start(d, carried):
+    def bulk_start(d):
         other, copy = bulk_copy(d)
 
         @pl.when(other != me)
         def _():
             copy.start()
 
-        return carried
-
-    lax.fori_loop(0, shares, bulk_start, 0)
+    each(0, shares, bulk_start)
     lambda_ref[...] = adjoint
-
-    own = lax.div(me, shares) == b
+    lambda_copy = pltpu.make_async_copy(lambda_ref, lambda_any, lambda_sem)
+    lambda_copy.start()
+
+    own = div(me, shares) == b
 
     @pl.when(own)
     def _():
@@ -383,7 +410,7 @@
     enter_send[...] = entering
 
     def enter_copy(d):
-        share = lax.rem(mine + d, shares)
+        share = rem(mine + d, shares)
         other = b * shares + share
         return other, pltpu.make_async_remote_copy(
             src_ref=enter_send,
@@ -391,21 +418,19 @@
             send_sem=enter_send_sem.at[share],
             recv_sem=enter_recv_sem.at[mine],
             device_id=(
-                lax.div(other, n_gy * n_gz), lax.rem(lax.div(other, n_gz), n_gy), lax.rem(other, n_gz)
+                div(other, n_gy * n_gz), rem(div(other, n_gz), n_gy), rem(other, n_gz)
             ),
             device_id_type=MESH,
         )
 
-    def enter_start(d, carried):
+    def enter_start(d):
         other, copy = enter_copy(d)
 
         @pl.when(other != me)
         def _():
             copy.start()
 
-        return carried
-
-    lax.fori_loop(0, shares, enter_start, 0)
+    each(0, shares, enter_start)
 
     @pl.when(own)
     def _():
@@ -421,7 +446,7 @@
         def _():
             copy.wait_send()
 
-    at_y = lax.rem(me, shares) * y_rows + iota((pad_rows, LANES), 0)
+    at_y = rem(me, shares) * y_rows + iota((pad_rows, LANES), 0)
     from_low = jnp.exp(at_y.astype(jnp.float32) * (-1.0 / length))
     from_high = jnp.exp(jnp.maximum(brick_y - 1 - at_y, 0).astype(jnp.float32) * (-1.0 / length))
     for i in range(n_gx):
@@ -458,7 +483,7 @@
         product = dot(high, block_high, NN) + dot(low, block_high, NN) + dot(high, block_low, NN)
         wide_ref[...] = product if i == 0 else wide_ref[...] + product
 
-    def bulk_sent(d, carried):
+    def bulk_sent(d):
         other, copy = bulk_copy(d)
         _, enter = enter_copy(d)
 
@@ -467,10 +492,9 @@
             copy.wait_send()
             enter.wait_send()
 
-        return carried
-
-    lax.fori_loop(0, shares, bulk_sent, 0)
-    lax.fori_loop(1, groups, well_sent, 0)
+    each(0, shares, bulk_sent)
+    each(1, groups, well_sent)
+    lambda_copy.wait()
 
 
 def depth_kernel(
@@ -534,9 +558,15 @@
             jax.ShapeDtypeStruct((lines, brick_y), f32),
             jax.ShapeDtypeStruct((n_gz * tiles * pad_rows, tile_z * wide_x), f32),
         ),
-        in_specs=[vmem, vmem, vmem, away, away, away],
-        out_specs=(vmem, vmem),
+        in_specs=[away] * 6,
+        out_specs=(away, vmem),
         scratch_shapes=[
+            pltpu.VMEM((lines, brick_y), f32),
+            dma,
+            pltpu.VMEM((brick_z, wells), f32),
+            pltpu.VMEM((1, wells), jnp.int32),
+            pltpu.VMEM((1, wells), jnp.int32),
+            dma((3,)),
             pltpu.VMEM((steps, lines, brick_y), jnp.int32),
             pltpu.VMEM(field, f32),
             pltpu.VMEM((steps, lines, brick_y), f32),
@@ -572,6 +602,8 @@
             dma((shares,)),
             pltpu.VMEM((n_gx * LANES, tile_z * wide_x), jnp.bfloat16),
             pltpu.VMEM((n_gx * LANES, tile_z * wide_x), jnp.bfloat16),
+            pltpu.VMEM((shares * pad_rows, brick_y), jnp.bfloat16),
+            pltpu.VMEM((shares * pad_rows, brick_y), jnp.bfloat16),
         ],
         compiler_params=pltpu.CompilerParams(
             collective_id=0, has_side_effects=True, vmem_limit_bytes=56 * 2**20

time: 38.7 us -> 37.6 us (0.972)
  Pallas kernels: 37.9 us -> 36.8 us
    pallas_call x1, Pallas kernels: 35.5 us -> 34.5 us  [per_device(): run(well_sources.T, well_owner.reshape(1, wells), well_cell.reshape(1, we...]
where the time goes in v1:
time: 37.6 us; the launch traced here: 37.5 us
  Pallas kernels  36.8 us (98%)
  between operations  0.64 us (2%)
    pallas_call x1, Pallas kernels, per_device(): run(well_sources.T, well_owner.reshape(1, wells), well_cell.reshape(1, we...  34.5 us
    pallas_call x1, Pallas kernels, per_device(): pl.pallas_call(functools.partial(depth_kernel, depth_sizes), out_shape=(j...  2.37 us

profile of v1, /device:TPU:0, one launch (start us, length us, event | category | flops | bytes accessed | tf_op | source)
XLA Modules:
  0.0 37.5 jit_solution(15315646790716930203)
XLA Ops:
  0.6 34.5 %shard_map.77 = (f32[512,128]{1,0:T(8,128)}, f32[128,1024]{1,0:T(8,128)}) custom-call(f32[32,96]{1,0:T(8,128)} %bitcast.11, s32[1,96]{1,0:T(1,128)} %bitcast.12, s32[1,96]{1,0:T(1,128)} %bitcast.13, s32[3,512,128]{2,1,0:T(8,128)} %bitcast.8, f32[3,512,128]{2,1,0:T(8,128)} %bitcast.9, f32[3,512,128]{2,1,0:T(8,128)} %bitcast.10), custom_call_target="tpu_custom_call" | custom-call | tf_op jit(solution)/shard_map/pallas_call | solution.py:612
  35.1 2.4 %shard_map.78 = (f32[512,128]{1,0:T(8,128)}, f32[1024,64]{1,0:T(8,128)}) custom-call(f32[512,128]{1,0:T(8,128)} %get-tuple-element.6.lambda_ref, f32[128,1024]{1,0:T(8,128)} %get-tuple-element.7.wide_ref), custom_call_target="tpu_custom_call" | custom-call | tf_op jit(solution)/shard_map/pallas_call | solution.py:621

commit v2 on v1

--- a/solution.py
+++ b/solution.py
@@ -71,7 +71,7 @@
     source_ref, owner_ref, cell_ref, small_sem,
     flow_ref, courant_ref, tracer_ref, load_sem,
     payload_ref, well_send, well_recv, well_send_sem, well_recv_sem,
-    rise_ref, fall_ref, sum_ref, grad_ref,
+    sum_ref, grad_ref,
     x_send, x_recv, y_send, y_recv, z_send, z_recv, face_send_sem, face_recv_sem,
     carry_send, carry_recv, carry_send_sem, carry_recv_sem,
     enter_send, enter_recv, enter_send_sem, enter_recv_sem,
@@ -195,7 +195,10 @@
     shape = (shares * pad_rows, brick_y)
     near = jnp.abs(line_place(iota(shape, 0)) - iota(shape, 1)).astype(jnp.float32)
     table_y = jnp.exp(near * (-1.0 / length)) / math.sqrt(length)
-    y_high[...], y_low[...] = parts(table_y)
+    take_row, take_lane = iota((2 * ROWS, brick_y), 0), iota((2 * ROWS, brick_y), 1)
+    from_end = jnp.where(take_row < ROWS, brick_y - take_lane, take_lane + 1)
+    pull = jnp.exp(from_end.astype(jnp.float32) * (-1.0 / length)) / math.sqrt(length)
+    y_high[...], y_low[...] = parts(jnp.concatenate([table_y, pull], axis=0))
 
     spread = flag(div(iota((lines, LANES), 0), brick_x) == iota((lines, LANES), 1))
     x_pick = flag(iota((ROWS, LANES), 1) == brick_z)
@@ -223,7 +226,6 @@
 
     y_pos = iota((lines, brick_y), 1)
     x_pos = rem(iota((lines, brick_y), 0), brick_x)
-    take_row, take_lane = iota((2 * ROWS, brick_y), 0), iota((2 * ROWS, brick_y), 1)
     take = flag(
         ((take_row < ROWS) & (take_lane == 0)) | ((take_row >= ROWS) & (take_lane == brick_y - 1))
     )
@@ -263,30 +265,34 @@
         copies = face_copies(step)
         all_copies.extend(copies)
         flow_loads[step].wait()
+        sum_ref[...] = adjoint
+        last_x = pl.ds(brick_x - 1, brick_z, stride=brick_x)
+        first_x = pl.ds(0, brick_z, stride=brick_x)
+        last_z, first_z = pl.ds(lines - brick_x, brick_x), pl.ds(0, brick_x)
         flow = flow_ref[step]
-        flows = [courant_ref[axis] * adjoint for axis in range(3)]
-        rise = [
-            jnp.where((flow & (1 << axis)) != 0, flows[axis], 0.0) for axis in range(3)
-        ]
-        fall = [flows[axis] - rise[axis] for axis in range(3)]
-        z_send[step, 0] = rise[2][0:brick_x]
-        z_send[step, 1] = fall[2][lines - brick_x:lines]
-        when_start(*copies[4][:2])
-        when_start(*copies[5][:2])
-        rise_ref[...] = rise[0]
-        fall_ref[...] = fall[0]
-        x_send[step, 0] = rise_ref[pl.ds(0, brick_z, stride=brick_x), :]
-        x_send[step, 1] = fall_ref[pl.ds(brick_x - 1, brick_z, stride=brick_x), :]
-        when_start(*copies[0][:2])
-        when_start(*copies[1][:2])
-        edge = jnp.where(y_pos == 0, rise[1], jnp.where(y_pos == brick_y - 1, fall[1], 0.0))
+        flow_y = courant_ref[1] * adjoint
+        rise_y = jnp.where((flow & 2) != 0, flow_y, 0.0)
+        fall_y = flow_y - rise_y
+        edge = jnp.where(y_pos == 0, rise_y, jnp.where(y_pos == brick_y - 1, fall_y, 0.0))
         edge_high, edge_low = parts(edge)
         edge_rows = dot(take, edge_high, NT) + dot(take, edge_low, NT)
+        for axis, send, ends in ((0, x_send, (first_x, last_x)), (2, z_send, (first_z, last_z))):
+            for side, rows in enumerate(ends):
+                up = (flow_ref[step, rows, :] & (1 << axis)) != 0
+                leaving = up if side == 0 else jnp.logical_not(up)
+                send[step, side] = jnp.where(
+                    leaving, courant_ref[axis, rows, :] * sum_ref[rows, :], 0.0
+                )
         y_send[step, 0] = edge_rows[0:ROWS]
         y_send[step, 1] = edge_rows[ROWS:2 * ROWS]
-        when_start(*copies[2][:2])
-        when_start(*copies[3][:2])
-
+        for copy, sends, _ in copies:
+            when_start(copy, sends)
+
+        flow_x, flow_z = courant_ref[0] * adjoint, courant_ref[2] * adjoint
+        rise_x = jnp.where((flow & 1) != 0, flow_x, 0.0)
+        rise_z = jnp.where((flow & 4) != 0, flow_z, 0.0)
+        rise = [rise_x, rise_y, rise_z]
+        fall = [flow_x - rise_x, fall_y, flow_z - rise_z]
         rest = 1.0 - (courant_ref[0] + courant_ref[1] + courant_ref[2])
         updated = rest * adjoint
         updated = updated + jnp.where(
@@ -307,14 +313,10 @@
             def _():
                 copy.wait_recv()
 
-        top = pl.ds(brick_x - 1, brick_z, stride=brick_x)
-        bottom = pl.ds(0, brick_z, stride=brick_x)
-        sum_ref[top, :] = sum_ref[top, :] + x_recv[step, 0]
-        sum_ref[bottom, :] = sum_ref[bottom, :] + x_recv[step, 1]
-        last = pl.ds(lines - brick_x, brick_x)
-        sum_ref[last, :] = sum_ref[last, :] + z_recv[step, 0]
-        first = pl.ds(0, brick_x)
-        sum_ref[first, :] = sum_ref[first, :] + z_recv[step, 1]
+        for rows, recv, side in (
+            (last_x, x_recv, 0), (first_x, x_recv, 1), (last_z, z_recv, 0), (first_z, z_recv, 1)
+        ):
+            sum_ref[rows, :] = sum_ref[rows, :] + recv[step, side]
         side_rows = jnp.concatenate([y_recv[step, 0], y_recv[step, 1]], axis=0)
         side_high, side_low = parts(side_rows)
         adjoint = sum_ref[...] + (dot(side_high, put, TN) + dot(side_low, put, TN))
@@ -325,9 +327,12 @@
             gradient = grad_ref[...] + adjoint * tracer_ref[step]
         grad_ref[...] = gradient
 
-    from_end = jnp.where(take_row < ROWS, brick_y - take_lane, take_lane + 1)
-    pull = jnp.exp(from_end.astype(jnp.float32) * (-1.0 / length)) / math.sqrt(length)
-    carries = dot_three(pull, gradient, NT)
+    high, low = parts(gradient)
+    smooth_y = (
+        dot(y_high[...], high, NT) + dot(y_low[...], high, NT) + dot(y_high[...], low, NT)
+    )
+    bulk_send[...] = smooth_y[0:shares * pad_rows]
+    carries = smooth_y[shares * pad_rows:]
     packed = [
         carries[row:row + 1, t * LANES:(t + 1) * LANES] for row in (0, ROWS) for t in range(tiles)
     ]
@@ -356,15 +361,13 @@
             when_start(copy, sends)
             carry_copies.append((copy, sends, arrival, gets))
 
-    high, low = parts(gradient)
-    bulk_send[...] = (
-        dot(y_high[...], high, NT) + dot(y_low[...], high, NT) + dot(y_high[...], low, NT)
-    )
-
     mine = a * n_gz + c
 
+    def far_first(d):
+        return jnp.where(2 * b < n_gy, shares - 1 - d, d)
+
     def bulk_copy(d):
-        share = rem(mine + d, shares)
+        share = far_first(d)
         other = b * shares + share
         return other, pltpu.make_async_remote_copy(
             src_ref=bulk_send.at[pl.ds(pl.multiple_of(share * pad_rows, ROWS), pad_rows), :],
@@ -410,7 +413,7 @@
     enter_send[...] = entering
 
     def enter_copy(d):
-        share = rem(mine + d, shares)
+        share = far_first(d)
         other = b * shares + share
         return other, pltpu.make_async_remote_copy(
             src_ref=enter_send,
@@ -578,8 +581,6 @@
             dma((groups,)),
             pltpu.VMEM((lines, brick_y), f32),
             pltpu.VMEM((lines, brick_y), f32),
-            pltpu.VMEM((lines, brick_y), f32),
-            pltpu.VMEM((lines, brick_y), f32),
             pltpu.VMEM((steps, 2, brick_z, brick_y), f32),
             pltpu.VMEM((steps, 2, brick_z, brick_y), f32),
             pltpu.VMEM((steps, 2, ROWS, lines), f32),
@@ -602,8 +603,8 @@
             dma((shares,)),
             pltpu.VMEM((n_gx * LANES, tile_z * wide_x), jnp.bfloat16),
             pltpu.VMEM((n_gx * LANES, tile_z * wide_x), jnp.bfloat16),
-            pltpu.VMEM((shares * pad_rows, brick_y), jnp.bfloat16),
-            pltpu.VMEM((shares * pad_rows, brick_y), jnp.bfloat16),
+            pltpu.VMEM((shares * pad_rows + 2 * ROWS, brick_y), jnp.bfloat16),
+            pltpu.VMEM((shares * pad_rows + 2 * ROWS, brick_y), jnp.bfloat16),
         ],
         compiler_params=pltpu.CompilerParams(
             collective_id=0, has_side_effects=True, vmem_limit_bytes=56 * 2**20

time: 37.6 us -> 37.2 us (0.989)
  Pallas kernels: 36.8 us -> 36.4 us
    pallas_call x1, Pallas kernels: 34.5 us -> 34 us  [per_device(): run(well_sources.T, well_owner.reshape(1, wells), well_cell.reshape(1, we...]
where the time goes in v2:
time: 37.2 us; the launch traced here: 37 us
  Pallas kernels  36.4 us (98%)
  between operations  0.64 us (2%)
    pallas_call x1, Pallas kernels, per_device(): run(well_sources.T, well_owner.reshape(1, wells), well_cell.reshape(1, we...  34 us
    pallas_call x1, Pallas kernels, per_device(): pl.pallas_call(functools.partial(depth_kernel, depth_sizes), out_shape=(j...  2.37 us

profile of v2, /device:TPU:0, one launch (start us, length us, event | category | flops | bytes accessed | tf_op | source)
XLA Modules:
  0.0 37.0 jit_solution(7606580755096692068)
XLA Ops:
  0.6 34.0 %shard_map.77 = (f32[512,128]{1,0:T(8,128)}, f32[128,1024]{1,0:T(8,128)}) custom-call(f32[32,96]{1,0:T(8,128)} %bitcast.11, s32[1,96]{1,0:T(1,128)} %bitcast.12, s32[1,96]{1,0:T(1,128)} %bitcast.13, s32[3,512,128]{2,1,0:T(8,128)} %bitcast.8, f32[3,512,128]{2,1,0:T(8,128)} %bitcast.9, f32[3,512,128]{2,1,0:T(8,128)} %bitcast.10), custom_call_target="tpu_custom_call" | custom-call | tf_op jit(solution)/shard_map/pallas_call | solution.py:613
  34.6 2.4 %shard_map.78 = (f32[512,128]{1,0:T(8,128)}, f32[1024,64]{1,0:T(8,128)}) custom-call(f32[512,128]{1,0:T(8,128)} %get-tuple-element.6.lambda_ref, f32[128,1024]{1,0:T(8,128)} %get-tuple-element.7.wide_ref), custom_call_target="tpu_custom_call" | custom-call | tf_op jit(solution)/shard_map/pallas_call | solution.py:622

commit v3 on v2

--- a/solution.py
+++ b/solution.py
@@ -40,6 +40,10 @@
 def parts(value):
     high = value.astype(jnp.bfloat16)
     return high, (value - high.astype(jnp.float32)).astype(jnp.bfloat16)
+
+
+def lane_width(extent):
+    return extent if LANES % extent == 0 else round_up(extent, LANES)
 
 
 def dot(left, right, dims):
@@ -90,7 +94,7 @@
     wells = source_any.shape[1]
     full_z = n_gz * brick_z
     full_x = n_gx * brick_x
-    wide_x = round_up(full_x, LANES)
+    wide_x = lane_width(full_x)
     shares = n_gx * n_gz
     y_rows = brick_y // shares
     pad_rows = round_up(y_rows, ROWS)
@@ -178,16 +182,20 @@
     each(1, groups, well_start)
     well_recv[group_rows(group), :] = well_send[group_rows(group), :]
 
-    shape = (n_gx * LANES, wide_x)
+    block = max(wide_x, LANES)
+    shape = (n_gx * LANES, block)
     at_x = div(iota(shape, 0), LANES) * brick_x + rem(iota(shape, 0), brick_x)
-    far = jnp.abs(at_x - iota(shape, 1)).astype(jnp.float32)
+    to_x = rem(iota(shape, 1), wide_x) if wide_x < LANES else iota(shape, 1)
+    far = jnp.abs(at_x - to_x).astype(jnp.float32)
     table = jnp.exp(far * (-0.5 / brick_x)) / math.sqrt(2 * brick_x) / math.sqrt(2 * brick_z)
-    table = jnp.where(iota(shape, 1) < full_x, table, 0.0)
+    table = jnp.where(to_x < full_x, table, 0.0)
     depth_of = rem(div(iota(shape, 0), brick_x), tile_z)
-    for depth in range(tile_z):
-        high, low = parts(jnp.where(depth_of == depth, table, 0.0))
-        table_high[:, depth * wide_x:(depth + 1) * wide_x] = high
-        table_low[:, depth * wide_x:(depth + 1) * wide_x] = low
+    if wide_x < LANES:
+        depth_of = depth_of - div(iota(shape, 1), wide_x)
+    for start in range(0, tile_z * wide_x, block):
+        high, low = parts(jnp.where(depth_of == start // wide_x, table, 0.0))
+        table_high[:, start:start + block] = high
+        table_low[:, start:start + block] = low
 
     def line_place(row):
         return div(row, pad_rows) * y_rows + rem(row, pad_rows)
@@ -504,14 +512,16 @@
     sizes, lambda_ref, wide_ref, lambda_out, smooth_ref, stage_ref=None
 ):
     brick_z, full_z, full_x, y_rows, pad_rows, tile_z = sizes
-    wide_x = round_up(full_x, LANES)
+    wide_x = lane_width(full_x)
     lambda_out[...] = lambda_ref[...]
 
     fade = math.exp(-0.5 / brick_z)
 
     def plane(z):
         row, depth = z // tile_z * pad_rows, z % tile_z
-        return wide_ref[row:row + y_rows, depth * wide_x:(depth + 1) * wide_x]
+        start, shift = depth * wide_x // LANES * LANES, depth * wide_x % LANES
+        here = wide_ref[row:row + y_rows, start:start + max(wide_x, LANES)]
+        return pltpu.roll(here, LANES - shift, 1) if shift else here
 
     ahead = [plane(0)]
     for z in range(1, full_z):
@@ -543,7 +553,7 @@
     y_rows = brick_y // shares
     pad_rows = round_up(y_rows, ROWS)
     full_x, full_z = n_gx * brick_x, n_gz * brick_z
-    wide_x = round_up(full_x, LANES)
+    wide_x = lane_width(full_x)
     tile_z = LANES // brick_x
     tiles = lines // LANES
     f32 = jnp.float32

time: 37.2 us -> 36.5 us (0.981)
  Pallas kernels: 36.4 us -> 35.7 us
    pallas_call x1, Pallas kernels: 34 us -> 33.3 us  [per_device(): run(well_sources.T, well_owner.reshape(1, wells), well_cell.reshape(1, we...]
where the time goes in v3:
time: 36.5 us; the launch traced here: 36.3 us
  Pallas kernels  35.7 us (98%)
  between operations  0.64 us (2%)
    pallas_call x1, Pallas kernels, per_device(): run(well_sources.T, well_owner.reshape(1, wells), well_cell.reshape(1, we...  33.3 us
    pallas_call x1, Pallas kernels, per_device(): pl.pallas_call(functools.partial(depth_kernel, depth_sizes), out_shape=(j...  2.38 us

profile of v3, /device:TPU:0, one launch (start us, length us, event | category | flops | bytes accessed | tf_op | source)
XLA Modules:
  0.0 36.3 jit_solution(18323915407920518006)
XLA Ops:
  0.6 33.3 %shard_map.77 = (f32[512,128]{1,0:T(8,128)}, f32[128,512]{1,0:T(8,128)}) custom-call(f32[32,96]{1,0:T(8,128)} %bitcast.11, s32[1,96]{1,0:T(1,128)} %bitcast.12, s32[1,96]{1,0:T(1,128)} %bitcast.13, s32[3,512,128]{2,1,0:T(8,128)} %bitcast.8, f32[3,512,128]{2,1,0:T(8,128)} %bitcast.9, f32[3,512,128]{2,1,0:T(8,128)} %bitcast.10), custom_call_target="tpu_custom_call" | custom-call | tf_op jit(solution)/shard_map/pallas_call | solution.py:623
  33.9 2.4 %shard_map.78 = (f32[512,128]{1,0:T(8,128)}, f32[1024,64]{1,0:T(8,128)}) custom-call(f32[512,128]{1,0:T(8,128)} %get-tuple-element.6.lambda_ref, f32[128,512]{1,0:T(8,128)} %get-tuple-element.7.wide_ref), custom_call_target="tpu_custom_call" | custom-call | tf_op jit(solution)/shard_map/pallas_call | solution.py:632

commit v4 on v3

--- a/solution.py
+++ b/solution.py
@@ -341,6 +341,34 @@
     )
     bulk_send[...] = smooth_y[0:shares * pad_rows]
     carries = smooth_y[shares * pad_rows:]
+    mine = a * n_gz + c
+
+    def far_first(d):
+        return jnp.where(2 * b < n_gy, shares - 1 - d, d)
+
+    def bulk_copy(d):
+        share = far_first(d)
+        other = b * shares + share
+        return other, pltpu.make_async_remote_copy(
+            src_ref=bulk_send.at[pl.ds(pl.multiple_of(share * pad_rows, ROWS), pad_rows), :],
+            dst_ref=bulk_recv.at[mine],
+            send_sem=bulk_send_sem.at[share],
+            recv_sem=bulk_recv_sem.at[mine],
+            device_id=(
+                div(other, n_gy * n_gz), rem(div(other, n_gz), n_gy), rem(other, n_gz)
+            ),
+            device_id_type=MESH,
+        )
+
+    def bulk_start(d):
+        other, copy = bulk_copy(d)
+
+        @pl.when(other != me)
+        def _():
+            copy.start()
+
+    each(0, shares, bulk_start)
+
     packed = [
         carries[row:row + 1, t * LANES:(t + 1) * LANES] for row in (0, ROWS) for t in range(tiles)
     ]
@@ -369,33 +397,6 @@
             when_start(copy, sends)
             carry_copies.append((copy, sends, arrival, gets))
 
-    mine = a * n_gz + c
-
-    def far_first(d):
-        return jnp.where(2 * b < n_gy, shares - 1 - d, d)
-
-    def bulk_copy(d):
-        share = far_first(d)
-        other = b * shares + share
-        return other, pltpu.make_async_remote_copy(
-            src_ref=bulk_send.at[pl.ds(pl.multiple_of(share * pad_rows, ROWS), pad_rows), :],
-            dst_ref=bulk_recv.at[mine],
-            send_sem=bulk_send_sem.at[share],
-            recv_sem=bulk_recv_sem.at[mine],
-            device_id=(
-                div(other, n_gy * n_gz), rem(div(other, n_gz), n_gy), rem(other, n_gz)
-            ),
-            device_id_type=MESH,
-        )
-
-    def bulk_start(d):
-        other, copy = bulk_copy(d)
-
-        @pl.when(other != me)
-        def _():
-            copy.start()
-
-    each(0, shares, bulk_start)
     lambda_ref[...] = adjoint
     lambda_copy = pltpu.make_async_copy(lambda_ref, lambda_any, lambda_sem)
     lambda_copy.start()

time: 36.5 us -> 38.7 us (1.060)
  Pallas kernels: 35.7 us -> 37.9 us
    pallas_call x1, Pallas kernels: 33.3 us -> 35.6 us  [per_device(): run(well_sources.T, well_owner.reshape(1, wells), well_cell.reshape(1, we...]
where the time goes in v4:
time: 38.7 us; the launch traced here: 38.6 us
  Pallas kernels  37.9 us (98%)
  between operations  0.64 us (2%)
    pallas_call x1, Pallas kernels, per_device(): run(well_sources.T, well_owner.reshape(1, wells), well_cell.reshape(1, we...  35.6 us
    pallas_call x1, Pallas kernels, per_device(): pl.pallas_call(functools.partial(depth_kernel, depth_sizes), out_shape=(j...  2.38 us

profile of v4, /device:TPU:0, one launch (start us, length us, event | category | flops | bytes accessed | tf_op | source)
XLA Modules:
  0.0 38.6 jit_solution(3591189949696110810)
XLA Ops:
  0.6 35.6 %shard_map.77 = (f32[512,128]{1,0:T(8,128)}, f32[128,512]{1,0:T(8,128)}) custom-call(f32[32,96]{1,0:T(8,128)} %bitcast.11, s32[1,96]{1,0:T(1,128)} %bitcast.12, s32[1,96]{1,0:T(1,128)} %bitcast.13, s32[3,512,128]{2,1,0:T(8,128)} %bitcast.8, f32[3,512,128]{2,1,0:T(8,128)} %bitcast.9, f32[3,512,128]{2,1,0:T(8,128)} %bitcast.10), custom_call_target="tpu_custom_call" | custom-call | tf_op jit(solution)/shard_map/pallas_call | solution.py:624
  36.2 2.4 %shard_map.78 = (f32[512,128]{1,0:T(8,128)}, f32[1024,64]{1,0:T(8,128)}) custom-call(f32[512,128]{1,0:T(8,128)} %get-tuple-element.6.lambda_ref, f32[128,512]{1,0:T(8,128)} %get-tuple-element.7.wide_ref), custom_call_target="tpu_custom_call" | custom-call | tf_op jit(solution)/shard_map/pallas_call | solution.py:633
